TPU v7x, 32 devices: a whole 2x2x4 slice. The times are simulated.
32 devices in a mesh: freq: 4 (over x, core), col: 8 (over z, y).
Axes of the slice: x: 2, y: 2, z: 4, core: 2. Of those that a mesh axis runs over, the one named last changes fastest.
Arguments:
- spectra: bfloat16 [2, 8, 4096, 4096], P(None, None, 'freq', 'col'), may hold values from -0.62890625 to 0.62890625
- wavelet: float32 [2, 8], P(None, 'freq'), may hold values from -1.5 to 1.5
Outputs:
- predicted: bfloat16 [2, 8, 384, 4096], P(None, 'freq', None, 'col')
All inputs are finite; a program needn't handle non-finite values.
Results may differ from a plain program's by a relative error of at most 0.001.
Values may be sent and summed in bfloat16 or wider, within the bound.
A program may use at most 128 MiB of HBM per device.

v0:
```python
import jax
import jax.numpy as jnp
from jax import lax
from jax.sharding import PartitionSpec as P

NOUT = 384


def complex_product(left, right, form):
    real_part = jnp.einsum(
        form, left[0], right[0], preferred_element_type=jnp.float32
    ) - jnp.einsum(form, left[1], right[1], preferred_element_type=jnp.float32)
    imag_part = jnp.einsum(
        form, left[0], right[1], preferred_element_type=jnp.float32
    ) + jnp.einsum(form, left[1], right[0], preferred_element_type=jnp.float32)
    return jnp.stack([real_part, imag_part])


def predict(slab, window):
    upper = slab[:, :, :window, :]
    return complex_product(lax.all_gather(upper, "col", axis=3, tiled=True), slab, "fnw,fwc->fnc")


def local(spectra, wavelet):
    window = NOUT
    slab = lax.all_to_all(spectra, "freq", split_axis=1, concat_axis=2, tiled=True)
    product = predict(slab, window)
    wave_real = wavelet[0][:, None, None]
    wave_imag = wavelet[1][:, None, None]
    real_out = -(wave_real * product[0] - wave_imag * product[1])
    imag_out = -(wave_real * product[1] + wave_imag * product[0])
    return jnp.stack([real_out, imag_out]).astype(jnp.bfloat16)


def solution(mesh):
    return jax.shard_map(
        local,
        mesh=mesh,
        in_specs=(P(None, None, "freq", "col"), P(None, "freq")),
        out_specs=P(None, "freq", None, "col"),
        check_vma=False,
    )
```

profile of v0, /device:TPU:1, one launch (start us, length us, event | category | flops | bytes accessed | tf_op | source)
XLA Modules:
  0.0 421.9 jit_solution(6820030431905376740)
XLA Ops:
  6.5 0.0 all-gather.2.cloned.1.call-start
  6.5 8.0 %copy.4 = bf16[2,8,1024,512]{3,2,0,1:T(8,128)(2,1)S(1)} copy(bf16[2,8,1024,512]{3,2,1,0:T(8,128)(2,1)} %param.2) | data formatting | bytes 33554432 | tf_op args[0]
  14.6 186.0 %all_to_all.18 = bf16[2,8,1024,512]{3,2,0,1:T(8,128)(2,1)S(1)} all-to-all(bf16[2,8,1024,512]{3,2,0,1:T(8,128)(2,1)S(1)} %copy.4), channel_id=1, replica_groups=mesh['freq'=4,'col'=8] {'freq'}, dimensions={1} | all-to-all | bytes 33554432 | tf_op jit(solution)/shard_map/all_to_all | solution.py:26
  200.6 0.0 copy-start.2
  200.6 2.9 copy.8
  203.5 0.0 copy-start
  203.5 5.7 %copy-done = bf16[2,4,2,1024,512]{4,3,1,2,0:T(8,128)(2,1)} copy-done((bf16[2,4,2,1024,512]{4,3,1,2,0:T(8,128)(2,1)}, bf16[2,4,2,1024,512]{4,3,1,2,0:T(8,128)(2,1)S(1)}, u32[]{:S(2)}) %copy-start) | copy-done | bytes 16777240
  209.2 1.2 slice.34
  210.5 0.0 all-gather.2.cloned.1.call-update
  210.5 0.0 copy-done.2
  210.5 11.9 %fusion.8 = (bf16[1,2,4,1024,512]{4,3,2,1,0:T(8,128)(2,1)}, bf16[1,2,4,1024,512]{4,3,2,1,0:T(8,128)(2,1)}) fusion(bf16[2,2,4,1024,512]{4,3,2,1,0:T(8,128)(2,1)} %bitcast.34), kind=kLoop, calls=%fused_computation.16 | loop fusion | bytes 33554432 | tf_op jit(solution)/shard_map/slice | solution.py:12
  222.4 165.6 %all-gather.2.cloned.1.call-done = bf16[2,2,384,4096]{3,2,1,0:T(8,128)(2,1)} async-done(((bf16[2,2,384,512]{3,2,1,0:T(8,128)(2,1)}), bf16[2,2,384,4096]{3,2,1,0:T(8,128)(2,1)}) %all-gather.2.cloned.1.call-update) | async-done | bytes 12582928 | tf_op jit(solution)/shard_map/all_gather | solution.py:21
  388.0 0.0 copy-start.1
  388.0 7.8 %fusion.1 = f32[2,384,512]{2,1,0:T(8,128)S(1)} fusion(bf16[2,4096,512]{2,1,0:T(8,128)(2,1)} %bitcast.36, bf16[2,2,384,4096]{3,2,1,0:T(8,128)(2,1)} %all-gather.2.cloned.1.call-done), kind=kOutput, calls=%fused_computation.3 | convolution fusion | flops 3221225472 | bytes 16252928 | tf_op jit(solution)/shard_map/fnw,fwc->fnc/dot_general | solution.py:10
  395.8 0.0 copy-done.1
  395.8 0.0 slice-start
  395.8 5.6 %fusion = f32[2,384,512]{2,1,0:T(8,128)S(1)} fusion(bf16[2,4096,512]{2,1,0:T(8,128)(2,1)S(1)} %bitcast.40, bf16[2,2,384,4096]{3,2,1,0:T(8,128)(2,1)} %all-gather.2.cloned.1.call-done), kind=kOutput, calls=%fused_computation.2 | convolution fusion | flops 3221225472 | bytes 16252928 | tf_op jit(solution)/shard_map/fnw,fwc->fnc/dot_general | solution.py:13
  401.5 0.0 slice-start.1
  401.5 5.7 %fusion.4 = f32[2,384,512]{2,1,0:T(8,128)S(1)} fusion(f32[2,384,512]{2,1,0:T(8,128)S(1)} %fusion.1, bf16[2,4096,512]{2,1,0:T(8,128)(2,1)S(1)} %bitcast.41, bf16[2,2,384,4096]{3,2,1,0:T(8,128)(2,1)} %all-gather.2.cloned.1.call-done), kind=kOutput, calls=%fused_computation.9 | convolution fusion | flops 3221618688 | bytes 17825792 | tf_op jit(solution)/shard_map/fnw,fwc->fnc/dot_general | solution.py:12
  407.2 0.0 slice-done
  407.2 0.0 slice-done.1
  407.2 6.5 %fusion.6 = (bf16[1,2,384,512]{3,2,1,0:T(8,128)(2,1)S(1)}, bf16[1,2,384,512]{3,2,1,0:T(8,128)(2,1)S(1)}) fusion(f32[2,384,512]{2,1,0:T(8,128)S(1)} %fusion.4, f32[2]{0:T(128)S(1)} %get-tuple-element.12, f32[2]{0:T(128)S(1)} %get-tuple-element.11, f32[2,384,512]{2,1,0:T(8,128)S(1)} %fusion, bf16[2,4096,512]{2,1,0:T(8,128)(2,1)S(1)} %bitcast.39, ...), kind=kOutput, calls=%fused_computation.11 | convolution fusion | flops 3225550848 | bytes 19398672 | tf_op jit(solution)/shard_map/fnw,fwc->fnc/dot_general | solution.py:15
  413.7 1.3 pad_maximum_fusion
  (2 shorter events, 0.0 us)
Async XLA Ops:
  6.5 381.5 %all-gather.2.cloned.1.call-start = ((), (), s32[]{:S(2)}) async-start(), calls=%async_computation.1 | async-start | bytes 14155776 | tf_op jit(solution)/shard_map/all_gather | solution.py:21
  200.6 9.9 %copy-start.2 = (f32[2,2]{1,0:T(2,128)S(1)}, f32[2,2]{1,0:T(2,128)}, u32[]{:S(2)}) copy-start(f32[2,2]{1,0:T(2,128)} %param.3) | copy-start | bytes 52
  203.5 5.7 %copy-start = (bf16[2,4,2,1024,512]{4,3,1,2,0:T(8,128)(2,1)}, bf16[2,4,2,1024,512]{4,3,1,2,0:T(8,128)(2,1)S(1)}, u32[]{:S(2)}) copy-start(bf16[2,4,2,1024,512]{4,3,1,2,0:T(8,128)(2,1)S(1)} %copy.8) | copy-start | bytes 50331652
  388.0 7.8 %copy-start.1 = (bf16[1,2,4,1024,512]{4,3,2,1,0:T(8,128)(2,1)S(1)}, bf16[1,2,4,1024,512]{4,3,2,1,0:T(8,128)(2,1)}, u32[]{:S(2)}) copy-start(bf16[1,2,4,1024,512]{4,3,2,1,0:T(8,128)(2,1)} %get-tuple-element.5) | copy-start | bytes 25165828
  395.8 11.3 %slice-start = ((s8[8388608]{0:T(1024)(128)(4,1)}), s8[4194304]{0:T(1024)(128)(4,1)S(1)}, s32[]{:S(2)}) async-start(s8[8388608]{0:T(1024)(128)(4,1)} %bitcast.37), calls=%async_computation.2 | async-start | bytes 8388608
  401.5 5.7 %slice-start.1 = ((s8[8388608]{0:T(1024)(128)(4,1)}), s8[4194304]{0:T(1024)(128)(4,1)S(1)}, s32[]{:S(2)}) async-start(s8[8388608]{0:T(1024)(128)(4,1)} %bitcast.37), calls=%async_computation.3 | async-start | bytes 8388608
Sparse Core Ops, SparseCore 0:
  210.6 177.3 all-gather.1
where the time goes:
time: 423 us; the launch traced here: 422 us
  blocking collectives  186 us (44%)
  waiting for transfers between devices  166 us (39%)
  local copies, waits for them, and re-layouts  29.8 us (7%)
  matrix products  25.6 us (6%)
  between operations  13.5 us (3%)
    all_to_all x1, blocking collectives, local(): lax.all_to_all(spectra, 'freq', split_axis=1, concat_axis=2, tiled=True)  186 us
    all_gather x1, waiting for transfers between devices, predict(): lax.all_gather(upper, 'col', axis=3, tiled=True)  166 us
    unnamed x11, local copies, waits for them, and re-layouts  13.8 us
    slice x1, local copies, waits for them, and re-layouts, complex_product(): right[1]  11.9 us
  transfers between devices with their start and end apart: 1, of which 1 were waited for; matrix products, arithmetic and copies ran while one was open for 3% of the time, Pallas kernels for 0%

commit v1 on v0

v1 whole, which is shorter than its diff:
```python
import functools

import jax
import jax.numpy as jnp
from jax import lax
from jax.experimental import pallas as pl
from jax.experimental.pallas import tpu as pltpu
from jax.sharding import PartitionSpec as P

NOUT = 384
HALVES = 2
AHEAD = 3
LAG = 6
MESH = pl.DeviceIdType.MESH


def kernel(nf, ncol, spec, wave, out, upper, data, part, pair, far, data_sem, src_send, col_recv,
           up_send, down_send, y_send, y_recv, pair_send, pair_recv, far_send, far_recv):
    own = wave.shape[1]
    freqs, shots, width = spec.shape[1], spec.shape[2], spec.shape[3]
    ny = ncol // nf
    nz, nh = nf, nf // 2
    rows = NOUT // HALVES
    chunks = freqs * HALVES
    r, c = lax.axis_index("freq"), lax.axis_index("col")
    z, y = lax.div(c, ny), lax.rem(c, ny)
    h, k = lax.div(r, 2), lax.rem(r, 2)

    def at(freq, col):
        return {"freq": freq, "col": col}

    barrier = pltpu.get_barrier_semaphore()
    for d in range(1, nf):
        pl.semaphore_signal(barrier, inc=1, device_id=at(lax.rem(r + d, nf), c), device_id_type=MESH)
    for d in range(1, ny):
        pl.semaphore_signal(
            barrier, inc=1, device_id=at(r, z * ny + lax.rem(y + d, ny)), device_id_type=MESH
        )

    @pl.when(z > 0)
    def _():
        pl.semaphore_signal(barrier, inc=1, device_id=at(r, c - ny), device_id_type=MESH)

    @pl.when(z < nz - 1)
    def _():
        pl.semaphore_signal(barrier, inc=1, device_id=at(r, c + ny), device_id_type=MESH)

    def place(t):
        group, spot = lax.div(t, nf), lax.rem(t, nf)
        hh, kk = lax.rem(spot, nh), lax.div(spot, nh)
        f = (hh * 2 + kk) * own + lax.div(group, HALVES)
        return group, lax.rem(group, HALVES), hh, kk, f

    def source(t):
        _, half, _, _, f = place(t)
        return spec.at[:, f, pl.ds(pl.multiple_of(half * rows, rows), rows), :]

    def remote(src, dst, send, recv, device):
        return pltpu.make_async_remote_copy(
            src_ref=src, dst_ref=dst, send_sem=send, recv_sem=recv, device_id=device, device_id_type=MESH
        )

    def local_copy(t):
        return pltpu.make_async_copy(source(t), upper.at[y, t], col_recv.at[t])

    def source_copy(t):
        return remote(source(t), upper.at[y, t], src_send.at[t], col_recv.at[t], at(z, c))

    def up_copy(t):
        return remote(upper.at[y, t], upper.at[y, t], up_send.at[t], col_recv.at[t], at(r, c + ny))

    def down_copy(t):
        return remote(upper.at[y, t], upper.at[y, t], down_send.at[t], col_recv.at[t], at(r, c - ny))

    def y_copy(t, d):
        to = at(r, z * ny + lax.rem(y + d, ny))
        return remote(upper.at[y, t], upper.at[y, t], y_send.at[d - 1, t], y_recv.at[d - 1, t], to)

    def y_arrival(t, d):
        origin = lax.rem(y - d + ny, ny)
        block = upper.at[origin, t]
        return remote(block, block, y_send.at[d - 1, t], y_recv.at[d - 1, t], at(r, z * ny + origin))

    def pair_copy(t):
        group, _, hh, kk, _ = place(t)
        slot = group * nh + hh
        return remote(part.at[t], pair.at[slot], pair_send.at[t], pair_recv.at[slot], at(h * 2 + kk, c))

    def pair_arrival(t):
        group, _, hh, _, _ = place(t)
        slot = group * nh + hh
        return remote(part.at[t], pair.at[slot], pair_send.at[t], pair_recv.at[slot], at(h * 2 + 1 - k, c))

    def far_copy(t):
        group, _, hh, kk, _ = place(t)
        d = lax.rem(h - hh + nh, nh) - 1
        return remote(part.at[t], far.at[d, group], far_send.at[t], far_recv.at[d, group], at(hh * 2 + kk, c))

    def far_arrival(t, d):
        group, _, hh, kk, _ = place(t)
        origin = lax.rem(h + d + 1, nh) * 2 + k
        return remote(part.at[t], far.at[d, group], far_send.at[t], far_recv.at[d, group], at(origin, c))

    local_root = (r == 0) & (z == 0)
    sends_source = (r == 0) & (z > 0)
    goes_up = (z >= r) & (z < nz - 1)
    goes_down = (z <= r) & (z > 0)

    def start_source(t):
        @pl.when(local_root)
        def _():
            local_copy(t).start()

        @pl.when(sends_source)
        def _():
            source_copy(t).start()

    count = (nf - 1) + (ny - 1) + (z > 0).astype(jnp.int32) + (z < nz - 1).astype(jnp.int32)
    pl.semaphore_wait(barrier, count)

    for t in range(AHEAD):
        start_source(t)

    def load(f):
        return pltpu.make_async_copy(spec.at[:, f], data.at[f], data_sem.at[f])

    @pl.loop(0, freqs)
    def _(i):
        load(place(lax.rem(i, nf) + lax.div(i, nf) * nf * HALVES)[4]).start()

    def arrive(t):
        @pl.when(local_root)
        def _():
            local_copy(t).wait()

        @pl.when(jnp.logical_not(local_root))
        def _():
            down_copy(t).wait_recv()

        @pl.when(goes_up)
        def _():
            up_copy(t).start()

        @pl.when(goes_down)
        def _():
            down_copy(t).start()

        for d in range(1, ny):
            y_copy(t, d).start()

    def sent(t):
        @pl.when(sends_source)
        def _():
            source_copy(t).wait_send()

        @pl.when(goes_up)
        def _():
            up_copy(t).wait_send()

        @pl.when(goes_down)
        def _():
            down_copy(t).wait_send()

        for d in range(1, ny):
            y_copy(t, d).wait_send()

    def multiply(t):
        _, half, _, kk, f = place(t)
        for d in range(1, ny):
            y_arrival(t, d).wait_recv()

        @pl.when(half == 0)
        def _():
            load(f).wait()

        def dot(a, b):
            return jnp.dot(a, b, preferred_element_type=jnp.float32)

        tile = min(256, width)

        @pl.loop(0, width // tile)
        def _(j):
            columns = pl.ds(pl.multiple_of(j * tile, tile), tile)
            real, imag = None, None
            for b in range(ny):
                depth = slice(b * width, (b + 1) * width)
                ur, ui = upper[b, t, 0], upper[b, t, 1]
                dr, di = data[f, 0, depth, columns], data[f, 1, depth, columns]
                re = dot(ur, dr) - dot(ui, di)
                im = dot(ur, di) + dot(ui, dr)
                real = re if real is None else real + re
                imag = im if imag is None else imag + im
            part[t, 0, :, columns] = real
            part[t, 1, :, columns] = imag

        @pl.when(kk != k)
        def _():
            pair_copy(t).start()

    def join(t):
        group, _, hh, kk, _ = place(t)

        @pl.when(kk == k)
        def _():
            pair_arrival(t).wait_recv()
            part[t] = part[t] + pair[group * nh + hh]

            @pl.when(hh != h)
            def _():
                far_copy(t).start()

    def finish(t):
        group, half, hh, kk, _ = place(t)

        @pl.when(kk != k)
        def _():
            pair_copy(t).wait_send()

        @pl.when((kk == k) & (hh != h))
        def _():
            far_copy(t).wait_send()

        @pl.when((kk == k) & (hh == h))
        def _():
            for d in range(nh - 1):
                far_arrival(t, d).wait_recv()
            real, imag = part[t, 0], part[t, 1]
            for d in range(nh - 1):
                real = real + far[d, group, 0]
                imag = imag + far[d, group, 1]
            j = lax.div(group, HALVES)
            wr, wi = wave[0, j], wave[1, j]
            where = pl.ds(pl.multiple_of(half * rows, rows), rows)
            out[0, j, where, :] = (-(wr * real - wi * imag)).astype(out.dtype)
            out[1, j, where, :] = (-(wr * imag + wi * real)).astype(out.dtype)

    def within(t, fn):
        @pl.when((t >= 0) & (t < chunks))
        def _():
            fn(t)

    @pl.loop(0, chunks + LAG)
    def _(t):
        within(t - AHEAD, sent)

        @pl.when((t >= 1) & (t + AHEAD - 1 < chunks))
        def _():
            start_source(t + AHEAD - 1)

        within(t, arrive)
        within(t - 1, multiply)
        within(t - 2, join)
        within(t - LAG, finish)


def local(nf, ncol, spectra, wavelet):
    _, freqs, shots, width = spectra.shape
    own = wavelet.shape[1]
    rows, chunks = NOUT // HALVES, freqs * HALVES
    ny, nh = ncol // nf, nf // 2
    block = (2, rows, width)
    dma = pltpu.SemaphoreType.DMA
    return pl.pallas_call(
        functools.partial(kernel, nf, ncol),
        out_shape=jax.ShapeDtypeStruct((2, own, NOUT, width), jnp.bfloat16),
        in_specs=[pl.BlockSpec(memory_space=pl.ANY), pl.BlockSpec(memory_space=pltpu.SMEM)],
        out_specs=pl.BlockSpec(memory_space=pltpu.VMEM),
        scratch_shapes=[
            pltpu.VMEM((ny, chunks) + block, jnp.bfloat16),
            pltpu.VMEM((freqs, 2, shots, width), jnp.bfloat16),
            pltpu.VMEM((chunks,) + block, jnp.float32),
            pltpu.VMEM((chunks // 2,) + block, jnp.float32),
            pltpu.VMEM((nh - 1, chunks // nf) + block, jnp.float32),
            dma((freqs,)),
            dma((chunks,)),
            dma((chunks,)),
            dma((chunks,)),
            dma((chunks,)),
            dma((ny - 1, chunks)),
            dma((ny - 1, chunks)),
            dma((chunks,)),
            dma((chunks // 2,)),
            dma((chunks,)),
            dma((nh - 1, chunks // nf)),
        ],
        compiler_params=pltpu.CompilerParams(
            collective_id=0, has_side_effects=True, vmem_limit_bytes=58 * 2**20
        ),
        cost_estimate=pl.CostEstimate(
            flops=16 * freqs * NOUT * shots * width // 2, bytes_accessed=4 * freqs * shots * width, transcendentals=0
        ),
    )(spectra, wavelet)


def solution(mesh):
    return jax.shard_map(
        functools.partial(local, mesh.shape["freq"], mesh.shape["col"]),
        mesh=mesh,
        in_specs=(P(None, None, "freq", "col"), P(None, "freq")),
        out_specs=P(None, "freq", None, "col"),
        check_vma=False,
    )
```

time: 423 us -> 197 us (0.47)
  Pallas kernels: 0 us -> 194 us
  blocking collectives: 186 us -> 0 us
  waiting for transfers between devices: 166 us -> 0 us
  local copies, waits for them, and re-layouts: 29.8 us -> 2.65 us
  matrix products: 25.6 us -> 0 us
  between operations: 13.5 us -> 0.01 us
    pallas_call x0 -> x1, Pallas kernels: none -> 194 us  [local(): pl.pallas_call(functools.partial(kernel, nf, ncol), out_shape=jax.ShapeDt...]
    all_to_all x1 -> x0, blocking collectives: 186 us -> none  [local(): lax.all_to_all(spectra, 'freq', split_axis=1, concat_axis=2, tiled=True)]
    all_gather x1 -> x0, waiting for transfers between devices: 166 us -> none  [predict(): lax.all_gather(upper, 'col', axis=3, tiled=True)]
    dot_general x4 -> x0, matrix products: 25.6 us -> none  [the longest x1 7.79 us: complex_product(): jnp.einsum(form, left[0], right[0], preferred_element_type=jnp.float32)]
    slice x2 -> x0, local copies, waits for them, and re-layouts: 13.1 us -> none  [the longest x1 11.9 us: complex_product(): right[1]]
    unnamed x11 -> x1, local copies, waits for them, and re-layouts: 13.8 us -> 2.65 us
  transfers between devices with their start and end apart: 1 -> 0, of which waited for: 1 -> 0; matrix products, arithmetic and copies ran while one was open for 3% -> 0% of each run, Pallas kernels for 0% -> 0%
where the time goes in v1:
time: 197 us
  Pallas kernels  194 us (98%)
  local copies, waits for them, and re-layouts  2.65 us (1%)
    pallas_call x1, Pallas kernels, local(): pl.pallas_call(functools.partial(kernel, nf, ncol), out_shape=jax.ShapeDt...  194 us

profile of v1, /device:TPU:1, one launch (start us, length us, event | category | flops | bytes accessed | tf_op | source)
XLA Modules:
  0.0 196.9 jit_solution(3953645841008410471)
XLA Ops:
  0.0 194.2 %shard_map.28 = bf16[2,2,384,512]{3,2,1,0:T(8,128)(2,1)} custom-call(bf16[2,8,1024,512]{3,2,1,0:T(8,128)(2,1)} %spec.1, f32[2,2]{1,0:T(2,128)} %wave.1), custom_call_target="tpu_custom_call" | custom-call | flops 12884901888 | bytes 16777216 | tf_op jit(solution)/shard_map/pallas_call | solution.py:263
  194.2 2.7 %copy.4 = bf16[2,2,384,512]{3,2,1,0:T(8,128)(2,1)} copy(bf16[2,2,384,512]{3,2,1,0:T(8,128)(2,1)} %shard_map.28) | data formatting | bytes 3145728

commit v2 on v1

--- a/solution.py
+++ b/solution.py
@@ -8,9 +8,9 @@
 from jax.sharding import PartitionSpec as P
 
 NOUT = 384
-HALVES = 2
-AHEAD = 3
-LAG = 6
+HALVES = 4
+AHEAD = 6
+LAG = 11
 MESH = pl.DeviceIdType.MESH
 
 

time: 197 us -> 177 us (0.90)
  Pallas kernels: 194 us -> 174 us
    pallas_call x1, Pallas kernels: 194 us -> 174 us  [local(): pl.pallas_call(functools.partial(kernel, nf, ncol), out_shape=jax.ShapeDt...]
where the time goes in v2:
time: 177 us; the launch traced here: 176 us
  Pallas kernels  174 us (98%)
  local copies, waits for them, and re-layouts  2.65 us (1%)
    pallas_call x1, Pallas kernels, local(): pl.pallas_call(functools.partial(kernel, nf, ncol), out_shape=jax.ShapeDt...  174 us

profile of v2, /device:TPU:1, one launch (start us, length us, event | category | flops | bytes accessed | tf_op | source)
XLA Modules:
  0.0 176.4 jit_solution(17735752030453176338)
XLA Ops:
  0.0 173.7 %shard_map.28 = bf16[2,2,384,512]{3,2,1,0:T(8,128)(2,1)} custom-call(bf16[2,8,1024,512]{3,2,1,0:T(8,128)(2,1)} %spec.1, f32[2,2]{1,0:T(2,128)} %wave.1), custom_call_target="tpu_custom_call" | custom-call | flops 12884901888 | bytes 16777216 | tf_op jit(solution)/shard_map/pallas_call | solution.py:263
  173.7 2.7 %copy.4 = bf16[2,2,384,512]{3,2,1,0:T(8,128)(2,1)} copy(bf16[2,2,384,512]{3,2,1,0:T(8,128)(2,1)} %shard_map.28) | data formatting | bytes 3145728

commit v3 on v2

--- a/solution.py
+++ b/solution.py
@@ -8,9 +8,9 @@
 from jax.sharding import PartitionSpec as P
 
 NOUT = 384
-HALVES = 4
-AHEAD = 6
-LAG = 11
+HALVES = 6
+AHEAD = 4
+LAG = 10
 MESH = pl.DeviceIdType.MESH
 
 

time: 177 us -> 200 us (1.13)
  Pallas kernels: 174 us -> 198 us
    pallas_call x1, Pallas kernels: 174 us -> 198 us  [local(): pl.pallas_call(functools.partial(kernel, nf, ncol), out_shape=jax.ShapeDt...]
where the time goes in v3:
time: 200 us
  Pallas kernels  198 us (99%)
  local copies, waits for them, and re-layouts  2.65 us (1%)
    pallas_call x1, Pallas kernels, local(): pl.pallas_call(functools.partial(kernel, nf, ncol), out_shape=jax.ShapeDt...  198 us

profile of v3, /device:TPU:1, one launch (start us, length us, event | category | flops | bytes accessed | tf_op | source)
XLA Modules:
  0.0 200.3 jit_solution(14213331813004308950)
XLA Ops:
  0.0 197.6 %shard_map.28 = bf16[2,2,384,512]{3,2,1,0:T(8,128)(2,1)} custom-call(bf16[2,8,1024,512]{3,2,1,0:T(8,128)(2,1)} %spec.1, f32[2,2]{1,0:T(2,128)} %wave.1), custom_call_target="tpu_custom_call" | custom-call | flops 12884901888 | bytes 16777216 | tf_op jit(solution)/shard_map/pallas_call | solution.py:263
  197.6 2.7 %copy.4 = bf16[2,2,384,512]{3,2,1,0:T(8,128)(2,1)} copy(bf16[2,2,384,512]{3,2,1,0:T(8,128)(2,1)} %shard_map.28) | data formatting | bytes 3145728

commit v4 on v2

--- a/solution.py
+++ b/solution.py
@@ -9,7 +9,7 @@
 
 NOUT = 384
 HALVES = 4
-AHEAD = 6
+AHEAD = 16
 LAG = 11
 MESH = pl.DeviceIdType.MESH
 
@@ -239,7 +239,7 @@
         def _():
             fn(t)
 
-    @pl.loop(0, chunks + LAG)
+    @pl.loop(0, chunks + max(LAG, AHEAD))
     def _(t):
         within(t - AHEAD, sent)
 

time: 177 us -> 176 us (level)
  no operation moved by 1% of the time
where the time goes in v4:
time: 176 us
  Pallas kernels  173 us (98%)
  local copies, waits for them, and re-layouts  2.65 us (2%)
    pallas_call x1, Pallas kernels, local(): pl.pallas_call(functools.partial(kernel, nf, ncol), out_shape=jax.ShapeDt...  173 us

profile of v4, /device:TPU:1, one launch (start us, length us, event | category | flops | bytes accessed | tf_op | source)
XLA Modules:
  0.0 175.7 jit_solution(11558188112143410854)
XLA Ops:
  0.0 173.0 %shard_map.28 = bf16[2,2,384,512]{3,2,1,0:T(8,128)(2,1)} custom-call(bf16[2,8,1024,512]{3,2,1,0:T(8,128)(2,1)} %spec.1, f32[2,2]{1,0:T(2,128)} %wave.1), custom_call_target="tpu_custom_call" | custom-call | flops 12884901888 | bytes 16777216 | tf_op jit(solution)/shard_map/pallas_call | solution.py:263
  173.0 2.7 %copy.4 = bf16[2,2,384,512]{3,2,1,0:T(8,128)(2,1)} copy(bf16[2,2,384,512]{3,2,1,0:T(8,128)(2,1)} %shard_map.28) | data formatting | bytes 3145728

commit v5 on v4

--- a/solution.py
+++ b/solution.py
@@ -9,6 +9,7 @@
 
 NOUT = 384
 HALVES = 4
+PIECES = 2
 AHEAD = 16
 LAG = 11
 MESH = pl.DeviceIdType.MESH
@@ -22,6 +23,7 @@
     nz, nh = nf, nf // 2
     rows = NOUT // HALVES
     chunks = freqs * HALVES
+    small, pieces = rows // PIECES, chunks * PIECES
     r, c = lax.axis_index("freq"), lax.axis_index("col")
     z, y = lax.div(c, ny), lax.rem(c, ny)
     h, k = lax.div(r, 2), lax.rem(r, 2)
@@ -51,9 +53,14 @@
         f = (hh * 2 + kk) * own + lax.div(group, HALVES)
         return group, lax.rem(group, HALVES), hh, kk, f
 
-    def source(t):
-        _, half, _, _, f = place(t)
-        return spec.at[:, f, pl.ds(pl.multiple_of(half * rows, rows), rows), :]
+    def source(s):
+        _, half, _, _, f = place(lax.div(s, PIECES))
+        first = pl.multiple_of(half * rows + lax.rem(s, PIECES) * small, small)
+        return spec.at[:, f, pl.ds(first, small), :]
+
+    def piece(b, s):
+        first = pl.multiple_of(lax.rem(s, PIECES) * small, small)
+        return upper.at[b, lax.div(s, PIECES), :, pl.ds(first, small), :]
 
     def remote(src, dst, send, recv, device):
         return pltpu.make_async_remote_copy(
@@ -61,24 +68,24 @@
         )
 
     def local_copy(t):
-        return pltpu.make_async_copy(source(t), upper.at[y, t], col_recv.at[t])
+        return pltpu.make_async_copy(source(t), piece(y, t), col_recv.at[t])
 
     def source_copy(t):
-        return remote(source(t), upper.at[y, t], src_send.at[t], col_recv.at[t], at(z, c))
+        return remote(source(t), piece(y, t), src_send.at[t], col_recv.at[t], at(z, c))
 
     def up_copy(t):
-        return remote(upper.at[y, t], upper.at[y, t], up_send.at[t], col_recv.at[t], at(r, c + ny))
+        return remote(piece(y, t), piece(y, t), up_send.at[t], col_recv.at[t], at(r, c + ny))
 
     def down_copy(t):
-        return remote(upper.at[y, t], upper.at[y, t], down_send.at[t], col_recv.at[t], at(r, c - ny))
+        return remote(piece(y, t), piece(y, t), down_send.at[t], col_recv.at[t], at(r, c - ny))
 
     def y_copy(t, d):
         to = at(r, z * ny + lax.rem(y + d, ny))
-        return remote(upper.at[y, t], upper.at[y, t], y_send.at[d - 1, t], y_recv.at[d - 1, t], to)
+        return remote(piece(y, t), piece(y, t), y_send.at[d - 1, t], y_recv.at[d - 1, t], to)
 
     def y_arrival(t, d):
         origin = lax.rem(y - d + ny, ny)
-        block = upper.at[origin, t]
+        block = piece(origin, t)
         return remote(block, block, y_send.at[d - 1, t], y_recv.at[d - 1, t], at(r, z * ny + origin))
 
     def pair_copy(t):
@@ -167,7 +174,8 @@
     def multiply(t):
         _, half, _, kk, f = place(t)
         for d in range(1, ny):
-            y_arrival(t, d).wait_recv()
+            for i in range(PIECES):
+                y_arrival(t * PIECES + i, d).wait_recv()
 
         @pl.when(half == 0)
         def _():
@@ -234,30 +242,35 @@
             out[0, j, where, :] = (-(wr * real - wi * imag)).astype(out.dtype)
             out[1, j, where, :] = (-(wr * imag + wi * real)).astype(out.dtype)
 
-    def within(t, fn):
-        @pl.when((t >= 0) & (t < chunks))
+    def within(t, fn, end):
+        @pl.when((t >= 0) & (t < end))
         def _():
             fn(t)
 
-    @pl.loop(0, chunks + max(LAG, AHEAD))
+    def move(s):
+        within(s - AHEAD, sent, pieces)
+
+        @pl.when((s >= 1) & (s + AHEAD - 1 < pieces))
+        def _():
+            start_source(s + AHEAD - 1)
+
+        within(s, arrive, pieces)
+
+    @pl.loop(0, chunks + max(LAG, AHEAD // PIECES))
     def _(t):
-        within(t - AHEAD, sent)
-
-        @pl.when((t >= 1) & (t + AHEAD - 1 < chunks))
-        def _():
-            start_source(t + AHEAD - 1)
-
-        within(t, arrive)
-        within(t - 1, multiply)
-        within(t - 2, join)
-        within(t - LAG, finish)
+        for i in range(PIECES - 1):
+            move(t * PIECES + i)
+        within(t - 1, multiply, chunks)
+        move(t * PIECES + PIECES - 1)
+        within(t - 2, join, chunks)
+        within(t - LAG, finish, chunks)
 
 
 def local(nf, ncol, spectra, wavelet):
     _, freqs, shots, width = spectra.shape
     own = wavelet.shape[1]
     rows, chunks = NOUT // HALVES, freqs * HALVES
-    ny, nh = ncol // nf, nf // 2
+    pieces, ny, nh = chunks * PIECES, ncol // nf, nf // 2
     block = (2, rows, width)
     dma = pltpu.SemaphoreType.DMA
     return pl.pallas_call(
@@ -272,12 +285,12 @@
             pltpu.VMEM((chunks // 2,) + block, jnp.float32),
             pltpu.VMEM((nh - 1, chunks // nf) + block, jnp.float32),
             dma((freqs,)),
-            dma((chunks,)),
-            dma((chunks,)),
-            dma((chunks,)),
-            dma((chunks,)),
-            dma((ny - 1, chunks)),
-            dma((ny - 1, chunks)),
+            dma((pieces,)),
+            dma((pieces,)),
+            dma((pieces,)),
+            dma((pieces,)),
+            dma((ny - 1, pieces)),
+            dma((ny - 1, pieces)),
             dma((chunks,)),
             dma((chunks // 2,)),
             dma((chunks,)),

time: 176 us -> 189 us (1.074)
  Pallas kernels: 173 us -> 186 us
    pallas_call x1, Pallas kernels: 173 us -> 186 us  [local(): pl.pallas_call(functools.partial(kernel, nf, ncol), out_shape=jax.ShapeDt...]
where the time goes in v5:
time: 189 us; the launch traced here: 188 us
  Pallas kernels  186 us (98%)
  local copies, waits for them, and re-layouts  2.65 us (1%)
    pallas_call x1, Pallas kernels, local(): pl.pallas_call(functools.partial(kernel, nf, ncol), out_shape=jax.ShapeDt...  186 us

profile of v5, /device:TPU:1, one launch (start us, length us, event | category | flops | bytes accessed | tf_op | source)
XLA Modules:
  0.0 188.4 jit_solution(11521099389373037384)
XLA Ops:
  0.0 185.7 %shard_map.28 = bf16[2,2,384,512]{3,2,1,0:T(8,128)(2,1)} custom-call(bf16[2,8,1024,512]{3,2,1,0:T(8,128)(2,1)} %spec.1, f32[2,2]{1,0:T(2,128)} %wave.1), custom_call_target="tpu_custom_call" | custom-call | flops 12884901888 | bytes 16777216 | tf_op jit(solution)/shard_map/pallas_call | solution.py:276
  185.7 2.7 %copy.4 = bf16[2,2,384,512]{3,2,1,0:T(8,128)(2,1)} copy(bf16[2,2,384,512]{3,2,1,0:T(8,128)(2,1)} %shard_map.28) | data formatting | bytes 3145728

commit v6 on v4

--- a/solution.py
+++ b/solution.py
@@ -10,7 +10,7 @@
 NOUT = 384
 HALVES = 4
 AHEAD = 16
-LAG = 11
+LAG = 16
 MESH = pl.DeviceIdType.MESH
 
 
@@ -239,6 +239,8 @@
         def _():
             fn(t)
 
+    late = chunks - 4
+
     @pl.loop(0, chunks + max(LAG, AHEAD))
     def _(t):
         within(t - AHEAD, sent)
@@ -249,7 +251,20 @@
 
         within(t, arrive)
         within(t - 1, multiply)
-        within(t - 2, join)
+
+        @pl.when(t < late)
+        def _():
+            within(t - 5, join)
+
+        @pl.when((t >= late) & (t < late + 3))
+        def _():
+            for i in range(2):
+                join(2 * (t - late) + late - 5 + i)
+
+        @pl.when(t >= late + 3)
+        def _():
+            within(t - 2, join)
+
         within(t - LAG, finish)
 
 

time: 176 us -> 173 us (0.983)
  Pallas kernels: 173 us -> 170 us
    pallas_call x1, Pallas kernels: 173 us -> 170 us  [local(): pl.pallas_call(functools.partial(kernel, nf, ncol), out_shape=jax.ShapeDt...]
where the time goes in v6:
time: 173 us; the launch traced here: 172 us
  Pallas kernels  170 us (98%)
  local copies, waits for them, and re-layouts  2.65 us (2%)
    pallas_call x1, Pallas kernels, local(): pl.pallas_call(functools.partial(kernel, nf, ncol), out_shape=jax.ShapeDt...  170 us

profile of v6, /device:TPU:1, one launch (start us, length us, event | category | flops | bytes accessed | tf_op | source)
XLA Modules:
  0.0 172.4 jit_solution(17487469570527422935)
XLA Ops:
  0.0 169.7 %shard_map.28 = bf16[2,2,384,512]{3,2,1,0:T(8,128)(2,1)} custom-call(bf16[2,8,1024,512]{3,2,1,0:T(8,128)(2,1)} %spec.1, f32[2,2]{1,0:T(2,128)} %wave.1), custom_call_target="tpu_custom_call" | custom-call | flops 12884901888 | bytes 16777216 | tf_op jit(solution)/shard_map/pallas_call | solution.py:278
  169.7 2.7 %copy.4 = bf16[2,2,384,512]{3,2,1,0:T(8,128)(2,1)} copy(bf16[2,2,384,512]{3,2,1,0:T(8,128)(2,1)} %shard_map.28) | data formatting | bytes 3145728

commit v7 on v6

--- a/solution.py
+++ b/solution.py
@@ -8,9 +8,9 @@
 from jax.sharding import PartitionSpec as P
 
 NOUT = 384
-HALVES = 4
-AHEAD = 16
-LAG = 16
+HALVES = 6
+AHEAD = 24
+LAG = 24
 MESH = pl.DeviceIdType.MESH
 
 

time: 173 us -> 178 us (1.029)
  Pallas kernels: 170 us -> 175 us
    pallas_call x1, Pallas kernels: 170 us -> 175 us  [local(): pl.pallas_call(functools.partial(kernel, nf, ncol), out_shape=jax.ShapeDt...]
where the time goes in v7:
time: 178 us; the launch traced here: 177 us
  Pallas kernels  175 us (98%)
  local copies, waits for them, and re-layouts  2.65 us (1%)
    pallas_call x1, Pallas kernels, local(): pl.pallas_call(functools.partial(kernel, nf, ncol), out_shape=jax.ShapeDt...  175 us

profile of v7, /device:TPU:1, one launch (start us, length us, event | category | flops | bytes accessed | tf_op | source)
XLA Modules:
  0.0 177.4 jit_solution(10929405582764712005)
XLA Ops:
  0.0 174.7 %shard_map.28 = bf16[2,2,384,512]{3,2,1,0:T(8,128)(2,1)} custom-call(bf16[2,8,1024,512]{3,2,1,0:T(8,128)(2,1)} %spec.1, f32[2,2]{1,0:T(2,128)} %wave.1), custom_call_target="tpu_custom_call" | custom-call | flops 12884901888 | bytes 16777216 | tf_op jit(solution)/shard_map/pallas_call | solution.py:278
  174.7 2.7 %copy.4 = bf16[2,2,384,512]{3,2,1,0:T(8,128)(2,1)} copy(bf16[2,2,384,512]{3,2,1,0:T(8,128)(2,1)} %shard_map.28) | data formatting | bytes 3145728

commit v8 on v7

--- a/solution.py
+++ b/solution.py
@@ -8,9 +8,9 @@
 from jax.sharding import PartitionSpec as P
 
 NOUT = 384
-HALVES = 6
-AHEAD = 24
-LAG = 24
+HALVES = 3
+AHEAD = 12
+LAG = 12
 MESH = pl.DeviceIdType.MESH
 
 

time: 178 us -> 176 us (0.989)
  Pallas kernels: 175 us -> 173 us
where the time goes in v8:
time: 176 us
  Pallas kernels  173 us (98%)
  local copies, waits for them, and re-layouts  2.65 us (2%)
    pallas_call x1, Pallas kernels, local(): pl.pallas_call(functools.partial(kernel, nf, ncol), out_shape=jax.ShapeDt...  173 us

profile of v8, /device:TPU:1, one launch (start us, length us, event | category | flops | bytes accessed | tf_op | source)
XLA Modules:
  0.0 176.1 jit_solution(16557701276123078117)
XLA Ops:
  0.0 173.4 %shard_map.28 = bf16[2,2,384,512]{3,2,1,0:T(8,128)(2,1)} custom-call(bf16[2,8,1024,512]{3,2,1,0:T(8,128)(2,1)} %spec.1, f32[2,2]{1,0:T(2,128)} %wave.1), custom_call_target="tpu_custom_call" | custom-call | flops 12884901888 | bytes 16777216 | tf_op jit(solution)/shard_map/pallas_call | solution.py:278
  173.4 2.7 %copy.4 = bf16[2,2,384,512]{3,2,1,0:T(8,128)(2,1)} copy(bf16[2,2,384,512]{3,2,1,0:T(8,128)(2,1)} %shard_map.28) | data formatting | bytes 3145728
